TPU v7x, 128 devices: a whole 4x4x4 slice. The times are simulated.
128 devices in a mesh: grp: 16 (over x_hi, z, core), sp: 8 (over y, x_lo).
Axes of the slice: x: 4 (x_hi: 2, x_lo: 2; x = x_hi * 2 + x_lo), y: 4, z: 4, core: 2. Of those that a mesh axis runs over, the one named last changes fastest.
Arguments:
- hidden_states: bfloat16 [16, 1024, 5120], P('grp', 'sp'), may hold values from -6 to 6
- modulation: float32 [16, 2, 5120], P('grp'), may hold values from -3 to 3
- query_weight: bfloat16 [5120, 5120], P('grp', 'sp'), may hold values from -0.125 to 0.125
- key_weight: bfloat16 [5120, 5120], P('grp', 'sp'), may hold values from -0.125 to 0.125
- value_weight: bfloat16 [5120, 5120], P('grp', 'sp'), may hold values from -0.125 to 0.125
- query_mask: int32 [1280, 5120], P('grp', 'sp'), may hold values from 0 to 5
- key_mask: int32 [1280, 5120], P('grp', 'sp'), may hold values from 0 to 5
- value_mask: int32 [1280, 5120], P('grp', 'sp'), may hold values from 0 to 5
- query_gain: float32 [5120], P('sp'), may hold values from 1 to 12, as said below
- key_gain: float32 [5120], P('sp'), may hold values from 1 to 12, as said below
Outputs:
- attended: bfloat16 [16, 1024, 5120], P('grp', 'sp')
- gram: float32 [8, 640, 5120], P('sp', 'grp')
Inputs may be any that keep to these rules, and one draw needn't show every extreme that they name: `query_mask`: index of the kept pair of positions, in the order (0,1), (0,2), (0,3), (1,2), (1,3), (2,3). `key_mask`: index of the kept pair of positions, in the order (0,1), (0,2), (0,3), (1,2), (1,3), (2,3). `value_mask`: index of the kept pair of positions, in the order (0,1), (0,2), (0,3), (1,2), (1,3), (2,3). `query_gain`: positive gains. `key_gain`: positive gains.
All inputs are finite; a program needn't handle non-finite values.
Results may differ from a plain program's by a relative error of at most 0.017.
The roundings to bfloat16 on the way count: a program that leaves them out, or rounds other values in their place, can miss the bound.
Values may be sent and summed in bfloat16 or wider, within the bound.
No kernel may reach another device: no remote copies, remote signals or barrier semaphores. Data moves between devices by JAX's collectives and lax.ppermute only.
A program may use at most 128 MiB of HBM per device.

v0:
```python
import jax
import jax.numpy as jnp
from jax import lax
from jax.sharding import PartitionSpec as P

HEAD_DIM = 128
HEIGHT = 16
WIDTH = 16


def pair_tables(pair_index):
    first_slot = jnp.where(pair_index < 3, 0, jnp.where(pair_index < 5, 1, 2))
    second_slot = jnp.where(
        pair_index == 0, 1, jnp.where((pair_index == 1) | (pair_index == 3), 2, 3)
    )
    return (first_slot, second_slot)


def apply_mask(weight, mask_index):
    first_slot, second_slot = pair_tables(mask_index)
    slot_ids = jnp.arange(4, dtype=jnp.int32)[None, :, None]
    chosen = (first_slot[:, None, :] == slot_ids) | (second_slot[:, None, :] == slot_ids)
    chosen = chosen.reshape(weight.shape)
    return jnp.where(chosen, weight, jnp.zeros((), jnp.bfloat16))


def add_rows(gathered, shard_piece):
    return jnp.dot(gathered, shard_piece, preferred_element_type=jnp.float32)


def rope_tables(seq_len, head_dim):
    positions = jnp.arange(seq_len, dtype=jnp.int32)
    frame_pos = (positions // (HEIGHT * WIDTH)).astype(jnp.float32)
    row_pos = (positions // WIDTH % HEIGHT).astype(jnp.float32)
    col_pos = (positions % WIDTH).astype(jnp.float32)
    half_dim = head_dim // 2
    spatial = head_dim // 6
    temporal = half_dim - 2 * spatial
    pair_ids = jnp.arange(half_dim, dtype=jnp.int32)
    exponent = jnp.where(
        pair_ids < temporal,
        2.0 * pair_ids / (2.0 * temporal),
        jnp.where(
            pair_ids < temporal + spatial,
            2.0 * (pair_ids - temporal) / (2.0 * spatial),
            2.0 * (pair_ids - temporal - spatial) / (2.0 * spatial),
        ),
    ).astype(jnp.float32)
    frequency = jnp.power(jnp.float32(10000.0), -exponent)
    chosen_pos = jnp.where(
        pair_ids[None, :] < temporal,
        frame_pos[:, None],
        jnp.where(pair_ids[None, :] < temporal + spatial, row_pos[:, None], col_pos[:, None]),
    )
    angles = jnp.repeat(chosen_pos * frequency[None, :], 2, axis=1)
    return (jnp.cos(angles), jnp.sin(angles))


def swap_matrix(head_dim):
    entries = jnp.arange(head_dim, dtype=jnp.int32)
    source = entries[:, None]
    target = entries[None, :]
    negative = (target % 2 == 0) & (source == target + 1)
    positive = (target % 2 == 1) & (source == target - 1)
    return jnp.where(negative, -1.0, jnp.where(positive, 1.0, 0.0)).astype(jnp.float32)


def rotate_pairs(tensor, cosine_table, sine_table):
    swapped = jnp.einsum(
        "shd,de->she", tensor, swap_matrix(tensor.shape[-1]), precision=lax.Precision.HIGHEST
    )
    return tensor * cosine_table[:, None, :] + swapped * sine_table[:, None, :]


def layer_norm(states, shift_row, scale_row):
    values_f32 = states.astype(jnp.float32)
    average = jnp.mean(values_f32, axis=-1, keepdims=True)
    centred = values_f32 - average
    variance = jnp.mean(centred * centred, axis=-1, keepdims=True)
    return (centred * lax.rsqrt(variance + 1e-06) * (1.0 + scale_row) + shift_row).astype(
        jnp.bfloat16
    )


def attend(query_rot, key_rot, values_proj):
    seq_len, head_count, head_dim = query_rot.shape
    block_rows = min(512, seq_len)
    blocks = query_rot.reshape(seq_len // block_rows, block_rows, head_count, head_dim)

    def one_block(query_block):
        scores = jnp.einsum(
            "qhd,khd->hqk", query_block, key_rot, preferred_element_type=jnp.float32
        ) * head_dim ** (-0.5)
        top_score = jnp.max(scores, axis=-1, keepdims=True)
        expo_scores = jnp.exp(scores - top_score)
        probabilities = (expo_scores / jnp.sum(expo_scores, axis=-1, keepdims=True)).astype(
            jnp.bfloat16
        )
        return jnp.einsum(
            "hqk,khd->qhd", probabilities, values_proj, preferred_element_type=jnp.float32
        ).astype(jnp.bfloat16)

    outputs = lax.map(one_block, blocks)
    return outputs.reshape(seq_len, head_count * head_dim)


def per_device(
    hidden_states,
    modulation,
    query_weight,
    key_weight,
    value_weight,
    query_mask,
    key_mask,
    value_mask,
    query_gain,
    key_gain,
):
    normed = layer_norm(hidden_states[0], modulation[0, 0], modulation[0, 1])
    gathered = lax.all_gather(normed, "sp", axis=0, tiled=True)
    seq_len = gathered.shape[0]
    columns = query_weight.shape[1]
    masked_query = apply_mask(query_weight, query_mask)
    masked_key = apply_mask(key_weight, key_mask)
    masked_value = apply_mask(value_weight, value_mask)

    def add_one(piece):
        return add_rows(gathered, piece)

    queries = add_one(lax.all_gather(masked_query, "grp", axis=0, tiled=True))
    keys_proj = add_one(lax.all_gather(masked_key, "grp", axis=0, tiled=True))
    values_f32 = add_one(lax.all_gather(masked_value, "grp", axis=0, tiled=True))
    values_proj = values_f32.astype(jnp.bfloat16)
    squares = lax.psum(
        (jnp.sum(queries * queries, axis=1), jnp.sum(keys_proj * keys_proj, axis=1)), "sp"
    )
    model_width = columns * lax.axis_size("sp")
    queries = queries * lax.rsqrt(squares[0] / model_width + 1e-06)[:, None] * query_gain
    keys_proj = keys_proj * lax.rsqrt(squares[1] / model_width + 1e-06)[:, None] * key_gain
    heads_local = columns // HEAD_DIM
    cosine_table, sine_table = rope_tables(seq_len, HEAD_DIM)
    query_rot = rotate_pairs(
        queries.reshape(seq_len, heads_local, HEAD_DIM), cosine_table, sine_table
    ).astype(jnp.bfloat16)
    key_rot = rotate_pairs(
        keys_proj.reshape(seq_len, heads_local, HEAD_DIM), cosine_table, sine_table
    ).astype(jnp.bfloat16)
    attended = attend(query_rot, key_rot, values_proj.reshape(seq_len, heads_local, HEAD_DIM))
    token_major = lax.all_to_all(attended, "sp", split_axis=0, concat_axis=1, tiled=True)
    own_columns = lax.dynamic_slice_in_dim(gathered, lax.axis_index("sp") * columns, columns, 1)
    total_tokens = seq_len * lax.axis_size("grp")
    product = lax.dot_general(
        own_columns, gathered, (((0,), (0,)), ((), ())), preferred_element_type=jnp.float32
    )
    gram_rows = lax.psum_scatter(
        (product / total_tokens).astype(jnp.bfloat16), "grp", scatter_dimension=0, tiled=True
    ).astype(jnp.float32)
    return (token_major[None], gram_rows[None])


def solution(mesh):
    return jax.shard_map(
        per_device,
        mesh=mesh,
        in_specs=(
            P("grp", "sp", None),
            P("grp", None, None),
            P("grp", "sp"),
            P("grp", "sp"),
            P("grp", "sp"),
            P("grp", "sp"),
            P("grp", "sp"),
            P("grp", "sp"),
            P("sp"),
            P("sp"),
        ),
        out_specs=(P("grp", "sp", None), P("sp", "grp", None)),
        check_vma=False,
    )
```

profile of v0, /device:TPU:0, one launch (start us, length us, event | category | flops | bytes accessed | tf_op | source)
XLA Modules:
  0.0 529.9 jit_solution(16652227093056017946)
XLA Ops:
  7.2 0.9 slice_add_fusion
  8.2 1.6 convert_reduce_fusion
  9.8 1.9 fusion.30
  11.6 1.6 fusion.33
  13.3 0.0 all-gather.7.cloned.1.call-start
  13.4 0.1 select_select_fusion.5
  13.4 0.1 eq.225
  13.6 0.3 eq.226
  13.9 0.1 eq.234
  14.0 0.3 eq.235
  14.3 0.0 copy-done.8
  14.4 0.1 select_select_fusion.3
  14.4 0.1 eq.244
  14.6 0.3 eq.245
  14.9 0.1 eq.250
  15.0 1.2 eq.251
  16.2 1.0 select_select_fusion.1
  17.2 0.1 eq.253
  17.3 1.2 eq.254
  18.5 0.1 eq.259
  18.7 1.2 eq.260
  19.8 0.1 eq.228
  20.0 3.5 or_select_fusion
  23.5 0.0 all-gather.9.cloned.1.call-start
  23.5 0.7 all-gather.9.cloned.1.call-update
  24.2 0.5 all-gather.11.cloned.1.call-update
  24.8 0.0 reduce-scatter.2.cloned.1.call-start
  24.9 1.0 fusion.36
  25.9 0.2 broadcast_in_dim.185
  26.1 0.4 cos.16
  26.5 0.2 copy.36
  26.7 0.2 broadcast_in_dim.189
  26.9 0.4 sin.16
  27.2 1.0 copy.39
  28.2 195.3 %all-gather.5.cloned.1.call-done = bf16[1024,5120]{1,0:T(8,128)(2,1)} async-done(((bf16[128,5120]{1,0:T(8,128)(2,1)}), bf16[1024,5120]{1,0:T(8,128)(2,1)}) %all-gather.5.cloned.1.call-update) | async-done | bytes 10485776 | tf_op jit(solution)/shard_map/all_gather | solution.py:120
  223.6 12.0 %multiply_convert_fusion = bf16[640,5120]{1,0:T(8,128)(2,1)} fusion(bf16[1024,5120]{1,0:T(8,128)(2,1)} %all-gather.5.cloned.1.call-done, s32[]{:T(128)S(6)} %select_n.219), kind=kOutput, calls=%fused_computation.19 | convolution fusion | flops 6717440000 | bytes 18350084 | tf_op jit(solution)/shard_map/dot_general | solution.py:152
  235.7 56.8 %all-gather.7.cloned.1.call-done = bf16[5120,640]{1,0:T(8,128)(2,1)} async-done(((bf16[320,640]{1,0:T(8,128)(2,1)}), bf16[5120,640]{1,0:T(8,128)(2,1)}) %all-gather.7.cloned.1.call-update) | async-done | bytes 6553616 | tf_op jit(solution)/shard_map/all_gather | solution.py:130
  292.4 12.7 %multiply_reduce_fusion.2 = (f32[1024]{0:T(1024)S(1)}, f32[1024,640]{0,1:T(8,128)}) fusion(bf16[1024,5120]{1,0:T(8,128)(2,1)} %all-gather.5.cloned.1.call-done, bf16[5120,640]{1,0:T(8,128)(2,1)} %all-gather.7.cloned.1.call-done), kind=kOutput, calls=%fused_computation.34 | convolution fusion | flops 6712196096 | bytes 19664896 | tf_op jit(solution)/shard_map/dot_general | solution.py:28
  305.2 52.8 %all-gather.9.cloned.1.call-done = bf16[5120,640]{1,0:T(8,128)(2,1)} async-done(((bf16[320,640]{1,0:T(8,128)(2,1)}), bf16[5120,640]{1,0:T(8,128)(2,1)}) %all-gather.9.cloned.1.call-update) | async-done | bytes 6553616 | tf_op jit(solution)/shard_map/all_gather | solution.py:131
  358.0 12.8 %multiply_reduce_fusion.1 = (f32[1024]{0:T(1024)S(1)}, f32[1024,640]{0,1:T(8,128)}) fusion(bf16[1024,5120]{1,0:T(8,128)(2,1)} %all-gather.5.cloned.1.call-done, bf16[5120,640]{1,0:T(8,128)(2,1)} %all-gather.9.cloned.1.call-done), kind=kOutput, calls=%fused_computation.31 | convolution fusion | flops 6712196096 | bytes 19664896 | tf_op jit(solution)/shard_map/dot_general | solution.py:28
  370.8 19.1 %all-reduce = (f32[1024]{0:T(1024)S(1)}, f32[1024]{0:T(1024)S(1)}) all-reduce(f32[1024]{0:T(1024)S(1)} %get-tuple-element.81, f32[1024]{0:T(1024)S(1)} %get-tuple-element.83), channel_id=1, replica_groups=mesh['grp'=16,'sp'=8] {'sp'}, use_global_device_ids=true, to_apply=%region_3.4 | all-reduce | flops 2048 | bytes 16384 | tf_op jit(solution)/shard_map/psum | solution.py:134
  389.9 2.0 multiply_multiply_fusion
  392.0 2.4 copy.40
  394.4 2.0 multiply_multiply_fusion.1
  396.4 2.2 copy.37
  398.6 25.2 %all-gather.11.cloned.1.call-done = bf16[5120,640]{1,0:T(8,128)(2,1)} async-done(((bf16[320,640]{1,0:T(8,128)(2,1)}), bf16[5120,640]{1,0:T(8,128)(2,1)}) %all-gather.11.cloned.1.call-update) | async-done | bytes 6553616 | tf_op jit(solution)/shard_map/all_gather | solution.py:132
  423.8 12.5 %convolution_convert_fusion = bf16[1024,640]{0,1:T(8,128)(2,1)} fusion(bf16[1024,5120]{1,0:T(8,128)(2,1)} %all-gather.5.cloned.1.call-done, bf16[5120,640]{1,0:T(8,128)(2,1)} %all-gather.11.cloned.1.call-done), kind=kOutput, calls=%fused_computation.35 | convolution fusion | flops 6711541760 | bytes 18350080 | tf_op jit(solution)/shard_map/dot_general | solution.py:28
  436.3 2.5 copy.43
  438.8 8.5 %add_convert_fusion = bf16[1024,5,128]{2,0,1:T(8,128)(2,1)} fusion(f32[1024,5,128]{2,0,1:T(8,128)} %copy.40, f32[1024,5,128]{0,2,1:T(8,128)} %bitcast.83, f32[1024,128]{1,0:T(8,128)} %copy.39, f32[1024,128]{1,0:T(8,128)S(1)} %copy.36, s32[128]{0:T(128)S(1)} %get-tuple-element.91, s32[128]{0:T(128)S(1)} %get-tuple-element.92, ...), kind=kOutput, calls=%fused_computation.29 | convolution fusion | flops 1009352704 | bytes 7603456 | tf_op jit(solution)/shard_map/shd,de->she/dot_general | solution.py:69
  447.3 5.5 %add_convert_fusion.1 = bf16[1024,5,128]{2,0,1:T(8,128)(2,1)} fusion(f32[1024,5,128]{2,0,1:T(8,128)S(1)} %copy-done.2, f32[1024,5,128]{0,2,1:T(8,128)S(1)} %bitcast.81, f32[1024,128]{1,0:T(8,128)S(1)} %copy-done.3, f32[1024,128]{1,0:T(8,128)S(1)} %copy.36, s32[128]{0:T(128)S(1)} %get-tuple-element.91, s32[128]{0:T(128)S(1)} %get-tuple-element.92, ...), kind=kOutput, calls=%fused_computation.32 | convolution fusion | flops 1009352704 | bytes 7603456 | tf_op jit(solution)/shard_map/shd,de->she/dot_general | solution.py:69
  452.8 31.9 %while.10 = (s32[]{:T(128)}, bf16[2,512,5,128]{3,1,2,0:T(8,128)(2,1)}, bf16[2,512,5,128]{3,1,0,2:T(8,128)(2,1)}, bf16[1024,5,128]{2,0,1:T(8,128)(2,1)}, bf16[1024,5,128]{2,0,1:T(8,128)(2,1)}, /*index=5*/s32[]{:T(128)}) while((s32[]{:T(128)}, bf16[2,512,5,128]{3,1,2,0:T(8,128)(2,1)}, bf16[2,512,5,128]{3,1,0,2:T(8,128)(2,1)}, ...), condition=%wide.region_9.10_spmd, body=%wide.region_6.9_spmd.sunk | while | flops 1355613184 | bytes 40659612 | solution.py:103
  453.1 9.1 %fusion.109 = (f32[5,512]{1,0:T(8,128)S(1)}, f32[5,512,1024]{2,1,0:T(8,128)}) fusion(bf16[1024,5,128]{2,0,1:T(8,128)(2,1)} %get-tuple-element.145, bf16[2,512,5,128]{3,1,0,2:T(8,128)(2,1)} %get-tuple-element.144, s32[]{:T(128)} %get-tuple-element.136), kind=kOutput, calls=%fused_computation.123.clone.1 | convolution fusion | flops 678953984 | bytes 12462592 | tf_op jit(solution)/shard_map/while/body/eval_jaxpr/sub | solution.py:95
  462.2 5.7 %fusion.110 = bf16[2,512,5,128]{3,1,2,0:T(8,128)(2,1)S(1)} fusion(bf16[2,512,5,128]{3,1,2,0:T(8,128)(2,1)S(1)} %copy-done.4, s32[]{:T(128)} %get-tuple-element.136, bf16[1024,5,128]{2,0,1:T(8,128)(2,1)S(1)} %copy-done.6, f32[5,512,1024]{2,1,0:T(8,128)} %get-tuple-element.128, f32[5,512]{1,0:T(8,128)S(1)} %get-tuple-element.129), kind=kOutput, calls=%fused_computation.9.clone.1 | convolution fusion | flops 676659200 | bytes 12468228 | tf_op jit(solution)/shard_map/while/body/eval_jaxpr/hqk,khd->qhd/dot_general | solution.py:99
  467.9 1.0 copy-done.5
  469.0 8.8 %fusion.109 = (f32[5,512]{1,0:T(8,128)S(1)}, f32[5,512,1024]{2,1,0:T(8,128)}) fusion(bf16[1024,5,128]{2,0,1:T(8,128)(2,1)} %get-tuple-element.145, bf16[2,512,5,128]{3,1,0,2:T(8,128)(2,1)} %get-tuple-element.144, s32[]{:T(128)} %get-tuple-element.136), kind=kOutput, calls=%fused_computation.123.clone.1 | convolution fusion | flops 678953984 | bytes 12462592 | tf_op jit(solution)/shard_map/while/body/eval_jaxpr/sub | solution.py:95
  477.8 5.8 %fusion.110 = bf16[2,512,5,128]{3,1,2,0:T(8,128)(2,1)S(1)} fusion(bf16[2,512,5,128]{3,1,2,0:T(8,128)(2,1)S(1)} %copy-done.4, s32[]{:T(128)} %get-tuple-element.136, bf16[1024,5,128]{2,0,1:T(8,128)(2,1)S(1)} %copy-done.6, f32[5,512,1024]{2,1,0:T(8,128)} %get-tuple-element.128, f32[5,512]{1,0:T(8,128)S(1)} %get-tuple-element.129), kind=kOutput, calls=%fused_computation.9.clone.1 | convolution fusion | flops 676659200 | bytes 12468228 | tf_op jit(solution)/shard_map/while/body/eval_jaxpr/hqk,khd->qhd/dot_general | solution.py:99
  483.6 1.0 copy-done.5
  484.7 3.5 copy.44
  488.1 0.9 all_to_all.12
  489.0 0.2 copy.45
  489.2 27.5 %all_to_all.16 = bf16[8,128,640]{1,2,0:T(8,128)(2,1)S(1)} all-to-all(bf16[8,128,640]{1,2,0:T(8,128)(2,1)S(1)} %copy.45), channel_id=1, replica_groups=mesh['grp'=16,'sp'=8] {'sp'}, dimensions={0} | all-to-all | bytes 2621440 | tf_op jit(solution)/shard_map/all_to_all | solution.py:149
  516.7 1.4 copy.46
  518.2 2.8 reduce-scatter.2.cloned.1.call-done
  521.0 1.9 bitcast_convert_fusion
  (41 shorter events, 0.3 us)
Async XLA Ops:
  7.2 4.5 copy-start.1
  7.2 216.4 %all-gather.5.cloned.1.call-start = ((), (), s32[]{:S(2)}) async-start(), calls=%async_computation.2 | async-start | bytes 11796480 | tf_op jit(solution)/shard_map/all_gather | solution.py:120
  9.8 3.6 copy-start.7
  13.3 279.1 %all-gather.7.cloned.1.call-start = ((), (), s32[]{:S(2)}) async-start(), calls=%async_computation.3 | async-start | bytes 6963200 | tf_op jit(solution)/shard_map/all_gather | solution.py:130
  13.4 0.9 copy-start.8
  23.5 334.6 %all-gather.9.cloned.1.call-start = ((), (), s32[]{:S(2)}) async-start(), calls=%async_computation.4 | async-start | bytes 6963200 | tf_op jit(solution)/shard_map/all_gather | solution.py:131
  24.2 399.6 %all-gather.11.cloned.1.call-start = ((), (), s32[]{:S(2)}) async-start(), calls=%async_computation.5 | async-start | bytes 6963200 | tf_op jit(solution)/shard_map/all_gather | solution.py:132
  24.8 496.2 %reduce-scatter.2.cloned.1.call-start = ((), (), s32[]{:S(2)}) async-start(), calls=%async_computation.6 | async-start | bytes 6963200 | tf_op jit(solution)/shard_map/reduce_scatter | solution.py:155
  305.2 84.7 %copy-start.9 = (f32[640]{0:T(1024)S(1)}, f32[640]{0:T(1024)}, u32[]{:S(2)}) copy-start(f32[640]{0:T(1024)} %param.21) | copy-start | bytes 7684
  391.9 2.4 copy-start
  392.0 2.4 copy-start.10
  438.8 8.5 %copy-start.2 = (f32[1024,5,128]{2,0,1:T(8,128)S(1)}, f32[1024,5,128]{2,0,1:T(8,128)}, u32[]{:S(2)}) copy-start(f32[1024,5,128]{2,0,1:T(8,128)} %copy.37) | copy-start | bytes 7864324
  438.8 8.5 %copy-start.3 = (f32[1024,128]{1,0:T(8,128)S(1)}, f32[1024,128]{1,0:T(8,128)}, u32[]{:S(2)}) copy-start(f32[1024,128]{1,0:T(8,128)} %copy.39) | copy-start | bytes 1572868
  453.0 9.2 %copy-start.4 = (bf16[2,512,5,128]{3,1,2,0:T(8,128)(2,1)S(1)}, bf16[2,512,5,128]{3,1,2,0:T(8,128)(2,1)}, u32[]{:S(2)}) copy-start(bf16[2,512,5,128]{3,1,2,0:T(8,128)(2,1)} %get-tuple-element.137) | copy-start | bytes 3932164 | tf_op jit(solution)/shard_map/while
  453.0 9.2 %copy-start.6 = (bf16[1024,5,128]{2,0,1:T(8,128)(2,1)S(1)}, bf16[1024,5,128]{2,0,1:T(8,128)(2,1)}, u32[]{:S(2)}) copy-start(bf16[1024,5,128]{2,0,1:T(8,128)(2,1)} %get-tuple-element.146) | copy-start | bytes 3932164 | tf_op jit(solution)/shard_map/while
  467.9 1.1 copy-start.5
  469.0 8.8 %copy-start.4 = (bf16[2,512,5,128]{3,1,2,0:T(8,128)(2,1)S(1)}, bf16[2,512,5,128]{3,1,2,0:T(8,128)(2,1)}, u32[]{:S(2)}) copy-start(bf16[2,512,5,128]{3,1,2,0:T(8,128)(2,1)} %get-tuple-element.137) | copy-start | bytes 3932164 | tf_op jit(solution)/shard_map/while
  469.0 8.8 %copy-start.6 = (bf16[1024,5,128]{2,0,1:T(8,128)(2,1)S(1)}, bf16[1024,5,128]{2,0,1:T(8,128)(2,1)}, u32[]{:S(2)}) copy-start(bf16[1024,5,128]{2,0,1:T(8,128)(2,1)} %get-tuple-element.146) | copy-start | bytes 3932164 | tf_op jit(solution)/shard_map/while
  483.6 1.1 copy-start.5
Sparse Core Ops, SparseCore 0:
  13.4 210.1 all-gather.4
  226.1 66.3 all-gather.6
  294.9 63.0 all-gather.8
  360.3 63.4 all-gather.10
  427.9 93.0 reduce-scatter.1
where the time goes:
time: 536 us; the launch traced here: 530 us
  waiting for transfers between devices  334 us (62%)
  matrix products  93.5 us (17%)
  blocking collectives  46.7 us (9%)
  local copies, waits for them, and re-layouts  22.8 us (4%)
  other arithmetic  17.7 us (3%)
  between operations  14.5 us (3%)
    all_gather x1, waiting for transfers between devices, per_device(): gathered = lax.all_gather(normed, 'sp', axis=0, tiled=True)  195 us
    all_gather x1, waiting for transfers between devices, per_device(): queries = add_one(lax.all_gather(masked_query, 'grp', axis=0, tiled=True))  56.8 us
    all_gather x1, waiting for transfers between devices, per_device(): keys_proj = add_one(lax.all_gather(masked_key, 'grp', axis=0, tiled=True))  52.8 us
    dot_general x3, matrix products, add_rows(): return jnp.dot(gathered, shard_piece, preferred_element_type=jnp.float32)  38 us
    all_to_all x1, blocking collectives, per_device(): lax.all_to_all(attended, 'sp', split_axis=0, concat_axis=1, tiled=True)  27.5 us
    all_gather x1, waiting for transfers between devices, per_device(): lax.all_gather(masked_value, 'grp', axis=0, tiled=True)  25.2 us
    psum x1, blocking collectives, per_device(): lax.psum((jnp.sum(queries * queries, axis=1), jnp.sum(keys_proj * keys_pr...  19.1 us
    sub x2, matrix products, one_block(): expo_scores = jnp.exp(scores - top_score)  18 us
  transfers between devices with their start and end apart: 5, of which 5 were waited for; matrix products, arithmetic and copies ran while one was open for 23% of the time, Pallas kernels for 0%

commit v1 on v0

v1 whole, which is shorter than its diff:
```python
import functools

import jax
import jax.numpy as jnp
from jax import lax
from jax.experimental import pallas as pl
from jax.experimental.pallas import tpu as pltpu
from jax.sharding import Mesh
from jax.sharding import PartitionSpec as P

HEAD_DIM = 128
HEIGHT = 16
WIDTH = 16
XH, Z, C, Y, XL = 2, 4, 2, 4, 2
AXES = ("xh", "z", "c", "y", "xl")
TOK = 128
D = 5120
COLS = 640
ROWS = 320
HALF = D // 2
HEADS = 5
BF16, F32, I32 = jnp.bfloat16, jnp.float32, jnp.int32
MIB = 1 << 20


def linear(xh, z, c, y, xl):
    return (((xh * Z + z) * C + c) * Y + y) * XL + xl


def permute(x, move):
    pairs = []
    for xh in range(XH):
        for z in range(Z):
            for c in range(C):
                for y in range(Y):
                    for xl in range(XL):
                        pairs.append((linear(xh, z, c, y, xl), linear(*move(xh, z, c, y, xl))))
    return lax.ppermute(x, AXES, pairs)


def turn(c):
    return 1 if c == 0 else -1


def ring_y(x):
    return permute(x, lambda xh, z, c, y, xl: (xh, z, c, (y + turn(c)) % Y, xl))


def ring_z(x):
    return permute(x, lambda xh, z, c, y, xl: (xh, (z + turn(c)) % Z, c, y, xl))


def swap_xl(x):
    return permute(x, lambda xh, z, c, y, xl: (xh, z, c, y, 1 - xl))


def swap_xh(x):
    return permute(x, lambda xh, z, c, y, xl: (1 - xh, z, c, y, xl))


def swap_c(x):
    return permute(x, lambda xh, z, c, y, xl: (xh, z, 1 - c, y, xl))


def to_owner(x, s, dx):
    return permute(x, lambda xh, z, c, y, xl: (xh, z, c, (y - turn(c) * s) % Y, xl ^ dx))


def mask_kernel(wq, wk, wv, mq, mk, mv, out):
    group = lax.broadcasted_iota(I32, (ROWS, ROWS // 4), 0) // 4
    spread = (group == lax.broadcasted_iota(I32, (ROWS, ROWS // 4), 1)).astype(F32).astype(BF16)
    slot = lax.broadcasted_iota(I32, (ROWS, COLS), 0) % 4
    for i, (w, m) in enumerate(((wq, mq), (wk, mk), (wv, mv))):
        p = m[...]
        bits = jnp.where(p == 0, 3, jnp.where(p == 1, 5, jnp.where(p == 2, 9, jnp.where(p == 3, 6, jnp.where(p == 4, 10, 12)))))
        rows = jnp.dot(spread, bits.astype(F32).astype(BF16), preferred_element_type=F32).astype(I32)
        kept = (lax.shift_right_logical(rows, slot) & 1) == 1
        out[:, i * COLS : (i + 1) * COLS] = jnp.where(kept, w[...].astype(F32), 0.0).astype(BF16)


def masked_weights(wq, wk, wv, mq, mk, mv):
    return pl.pallas_call(
        mask_kernel,
        out_shape=jax.ShapeDtypeStruct((ROWS, 3 * COLS), BF16),
        compiler_params=pltpu.CompilerParams(vmem_limit_bytes=24 * MIB),
        cost_estimate=pl.CostEstimate(flops=10**8, bytes_accessed=3 * 10**6, transcendentals=0),
        name="masked_weights",
    )(wq, wk, wv, mq, mk, mv)


def norm_kernel(h, modulation, out):
    x = h[0].astype(F32)
    average = jnp.mean(x, axis=-1, keepdims=True)
    centred = x - average
    variance = jnp.mean(centred * centred, axis=-1, keepdims=True)
    scale = 1.0 + modulation[0, 1:2, :]
    out[...] = (centred * lax.rsqrt(variance + 1e-06) * scale + modulation[0, 0:1, :]).astype(BF16)


def layer_norm(h, modulation):
    rows = 32
    return pl.pallas_call(
        norm_kernel,
        out_shape=jax.ShapeDtypeStruct((TOK, D), BF16),
        grid=(TOK // rows,),
        in_specs=[pl.BlockSpec((1, rows, D), lambda i: (0, i, 0)), pl.BlockSpec((1, 2, D), lambda i: (0, 0, 0))],
        out_specs=pl.BlockSpec((rows, D), lambda i: (i, 0)),
        compiler_params=pltpu.CompilerParams(vmem_limit_bytes=24 * MIB),
        cost_estimate=pl.CostEstimate(flops=10**7, bytes_accessed=3 * 10**6, transcendentals=0),
        name="layer_norm",
    )(h, modulation)


def project_kernel(n_x, first, last, place, *refs):
    xs, refs = refs[:n_x], refs[n_x:]
    ws, refs = refs[:8], refs[8:]
    if not first:
        acc_in, refs = refs[0], refs[1:]
    if last:
        q_out, k_out, v_out, sq_out, x_v, w_v, sem_x, sem_w = refs
    else:
        acc_out, x_v, w_v, sem_x, sem_w = refs
    column = pl.multiple_of(place[0] * HALF, HALF)
    copies_w = []
    for j in range(8):
        row = pl.multiple_of(place[1 + j] * ROWS, ROWS)
        copies_w.append(pltpu.make_async_copy(ws[j], w_v.at[pl.ds(row, ROWS), :], sem_w.at[j]))
    copies_x = [
        pltpu.make_async_copy(xs[j].at[:, pl.ds(column, HALF)], x_v.at[j * TOK : (j + 1) * TOK, :], sem_x.at[j])
        for j in range(n_x)
    ]
    for copy in copies_w:
        copy.start()
    for copy in copies_x:
        copy.start()
    for copy in copies_w:
        copy.wait()
    for copy in copies_x:
        copy.wait()
    tile = 512

    @pl.loop(0, n_x * TOK // tile)
    def _(i):
        rows = pl.ds(pl.multiple_of(i * tile, tile), tile)
        x = x_v[rows, :]
        for part in range(3):
            cols = slice(part * COLS, (part + 1) * COLS)
            y = jnp.dot(x, w_v[:, cols], preferred_element_type=F32)
            if not first:
                y = y + acc_in[rows, cols]
            if not last:
                acc_out[rows, cols] = y
            elif part == 2:
                v_out[rows, :] = y.astype(BF16)
            else:
                (q_out if part == 0 else k_out)[rows, :] = y
                squares = y * y
                lanes = sum(squares[:, h * 128 : (h + 1) * 128] for h in range(HEADS))
                for b in range(tile // TOK):
                    line = jnp.sum(lanes[b * TOK : (b + 1) * TOK, :].T, axis=0, keepdims=True)
                    sq_out[place[9 + i * (tile // TOK) + b], part : part + 1, :] = line


def project(place, xs, ws, acc=None, last=False):
    n_x = len(xs)
    first = acc is None
    rows = n_x * TOK
    anywhere = pl.BlockSpec(memory_space=pl.ANY)
    vmem = pl.BlockSpec(memory_space=pltpu.VMEM)
    if last:
        out_shape = (
            jax.ShapeDtypeStruct((rows, COLS), F32),
            jax.ShapeDtypeStruct((rows, COLS), F32),
            jax.ShapeDtypeStruct((rows, COLS), BF16),
            jax.ShapeDtypeStruct((8, 8, TOK), F32),
        )
        out_specs = (vmem,) * 4
    else:
        out_shape = jax.ShapeDtypeStruct((rows, 3 * COLS), F32)
        out_specs = vmem
    return pl.pallas_call(
        functools.partial(project_kernel, n_x, first, last),
        out_shape=out_shape,
        in_specs=[pl.BlockSpec(memory_space=pltpu.SMEM)] + [anywhere] * (n_x + 8) + ([] if first else [vmem]),
        out_specs=out_specs,
        scratch_shapes=[
            pltpu.VMEM((rows, HALF), BF16),
            pltpu.VMEM((HALF, 3 * COLS), BF16),
            pltpu.SemaphoreType.DMA((n_x,)),
            pltpu.SemaphoreType.DMA((8,)),
        ],
        compiler_params=pltpu.CompilerParams(vmem_limit_bytes=48 * MIB),
        cost_estimate=pl.CostEstimate(
            flops=2 * rows * HALF * 3 * COLS, bytes_accessed=15 * 10**6, transcendentals=0
        ),
        name=f"project_{n_x}_{int(first)}_{int(last)}",
    )(place, *xs, *ws, *([] if first else [acc]))


def gram_kernel(tokens, place, *refs):
    xs, (out, x_v, own, o_v, sem_x, sem_o) = refs[:8], refs[8:]
    copies = [
        pltpu.make_async_copy(xs[j], x_v.at[j * TOK : (j + 1) * TOK, :], sem_x.at[j]) for j in range(8)
    ]
    for copy in copies:
        copy.start()
    for copy in copies:
        copy.wait()
    column = pl.multiple_of(place[0] * COLS, COLS)
    own[...] = x_v[:, pl.ds(column, COLS)].T

    @pl.loop(0, D // COLS)
    def _(i):
        cols = pl.ds(pl.multiple_of(i * COLS, COLS), COLS)
        slot = i % 2

        def send(j, at):
            to = pl.ds(pl.multiple_of(j * COLS, COLS), COLS)
            return pltpu.make_async_copy(o_v.at[at], out.at[:, to], sem_o.at[at])

        @pl.when(i >= 2)
        def _():
            send(i - 2, slot).wait()

        y = jnp.dot(own[...], x_v[:, cols], preferred_element_type=F32)
        o_v[slot] = (y * (1.0 / tokens)).astype(BF16)
        send(i, slot).start()

    for j in range(D // COLS - 2, D // COLS):
        to = slice(j * COLS, (j + 1) * COLS)
        pltpu.make_async_copy(o_v.at[j % 2], out.at[:, to], sem_o.at[j % 2]).wait()


def gram_rows(place, xs, tokens):
    anywhere = pl.BlockSpec(memory_space=pl.ANY)
    return pl.pallas_call(
        functools.partial(gram_kernel, tokens),
        out_shape=jax.ShapeDtypeStruct((COLS, D), BF16),
        in_specs=[pl.BlockSpec(memory_space=pltpu.SMEM)] + [anywhere] * 8,
        out_specs=anywhere,
        scratch_shapes=[
            pltpu.VMEM((8 * TOK, D), BF16),
            pltpu.VMEM((COLS, 8 * TOK), BF16),
            pltpu.VMEM((2, COLS, COLS), BF16),
            pltpu.SemaphoreType.DMA((8,)),
            pltpu.SemaphoreType.DMA((2,)),
        ],
        compiler_params=pltpu.CompilerParams(vmem_limit_bytes=40 * MIB),
        cost_estimate=pl.CostEstimate(flops=2 * COLS * 1024 * D, bytes_accessed=17 * 10**6, transcendentals=0),
        name="gram_rows",
    )(place, *xs)


def rope_tables(place):
    inside = jnp.arange(TOK, dtype=I32)[None, :]
    blocks = place[:, None]
    frame_pos = jnp.broadcast_to(blocks // 2, (8, TOK)).reshape(-1).astype(F32)
    row_pos = (blocks % 2 * 8 + inside // WIDTH).reshape(-1).astype(F32)
    col_pos = jnp.broadcast_to(inside % WIDTH, (8, TOK)).reshape(-1).astype(F32)
    half_dim = HEAD_DIM // 2
    spatial = HEAD_DIM // 6
    temporal = half_dim - 2 * spatial
    entry = jnp.arange(HEAD_DIM, dtype=I32)
    pair_ids = entry // 2
    exponent = jnp.where(
        pair_ids < temporal,
        2.0 * pair_ids / (2.0 * temporal),
        jnp.where(
            pair_ids < temporal + spatial,
            2.0 * (pair_ids - temporal) / (2.0 * spatial),
            2.0 * (pair_ids - temporal - spatial) / (2.0 * spatial),
        ),
    ).astype(F32)
    frequency = jnp.power(jnp.float32(10000.0), -exponent)
    chosen_pos = jnp.where(
        pair_ids[None, :] < temporal,
        frame_pos[:, None],
        jnp.where(pair_ids[None, :] < temporal + spatial, row_pos[:, None], col_pos[:, None]),
    )
    angles = chosen_pos * frequency[None, :]
    sine = jnp.sin(angles)
    even = (entry % 2 == 0)[None, :]
    return jnp.cos(angles), jnp.where(even, -sine, 0.0), jnp.where(even, 0.0, sine)


def attend_kernel(place, q_ref, k_ref, v_ref, *refs):
    squares, (gain_q, gain_k, cosine, sine_l, sine_r), outs = refs[:8], refs[8:13], refs[13:21]
    scale_v, k_v = refs[21:]

    @pl.when(pl.program_id(0) == 0)
    def _():
        total = squares[0][...]
        for other in squares[1:]:
            total = total + other[...]
        factor = lax.rsqrt(total / D + 1e-06)
        scale_v[2] = jnp.zeros((8 * TOK, TOK), F32)
        for b in range(8):
            scale_v[2, b * 8 : (b + 1) * 8, :] = factor[b]
        for b in range(8):
            source = place[b]
            for part in range(2):
                line = scale_v[2, pl.ds(source * 8 + part, 1), :]
                scale_v[part, b * TOK : (b + 1) * TOK, :] = jnp.broadcast_to(line, (TOK, TOK)).T

    def rotate(x, part, gain, rows):
        x = x * scale_v[part, rows, :] * gain
        left = pltpu.roll(x, HEAD_DIM - 1, 1)
        right = pltpu.roll(x, 1, 1)
        return (x * cosine[rows, :] + left * sine_l[rows, :] + right * sine_r[rows, :]).astype(BF16)

    every = slice(0, 8 * TOK)
    keys = rotate(k_ref[...], 1, gain_k[...], every)
    values = v_ref[...]
    factor = HEAD_DIM ** (-0.5) * 1.4426950408889634
    tile = 256
    for i in range(8 * TOK // tile):
        rows = slice(i * tile, (i + 1) * tile)
        q = rotate(q_ref[rows, :], 0, gain_q[...], rows)
        scores = lax.dot_general(q, keys, (((1,), (1,)), ((), ())), preferred_element_type=F32)
        top = jnp.max(scores, axis=-1, keepdims=True)
        weights = jnp.exp2((scores - top) * factor)
        total = jnp.sum(weights, axis=-1, keepdims=True)
        probabilities = (weights * (1.0 / total)).astype(BF16)
        out = jnp.dot(probabilities, values, preferred_element_type=F32).astype(BF16)
        for b in range(tile // TOK):
            outs[i * (tile // TOK) + b][...] = out[b * TOK : (b + 1) * TOK, :]


def attend(place, q, k, v, squares, gain_q, gain_k, tables):
    head = pl.BlockSpec((8 * TOK, HEAD_DIM), lambda h: (0, h))
    gain = pl.BlockSpec((1, HEAD_DIM), lambda h: (0, h))
    table = pl.BlockSpec((8 * TOK, HEAD_DIM), lambda h: (0, 0))
    square = pl.BlockSpec((8, 8, TOK), lambda h: (0, 0, 0))
    return pl.pallas_call(
        attend_kernel,
        out_shape=(jax.ShapeDtypeStruct((TOK, COLS), BF16),) * 8,
        grid=(HEADS,),
        in_specs=[pl.BlockSpec(memory_space=pltpu.SMEM), head, head, head]
        + [square] * 8
        + [gain, gain, table, table, table],
        out_specs=(pl.BlockSpec((TOK, HEAD_DIM), lambda h: (0, h)),) * 8,
        scratch_shapes=[pltpu.VMEM((3, 8 * TOK, TOK), F32), pltpu.VMEM((8 * TOK, HEAD_DIM), BF16)],
        compiler_params=pltpu.CompilerParams(vmem_limit_bytes=40 * MIB),
        cost_estimate=pl.CostEstimate(flops=4 * 1024 * 1024 * COLS, bytes_accessed=10**7, transcendentals=5 * 2**20),
        name="attend",
    )(place, q, k, v, *squares, gain_q[None], gain_k[None], *tables)


def gather_kernel(place, *refs):
    pieces, out, sem = refs[:8], refs[8], refs[9]
    copies = []
    for j in range(8):
        column = pl.multiple_of(place[j] * COLS, COLS)
        copies.append(pltpu.make_async_copy(pieces[j], out.at[0, :, pl.ds(column, COLS)], sem.at[j]))
    for copy in copies:
        copy.start()
    for copy in copies:
        copy.wait()


def gather_columns(place, pieces):
    anywhere = pl.BlockSpec(memory_space=pl.ANY)
    return pl.pallas_call(
        gather_kernel,
        out_shape=jax.ShapeDtypeStruct((1, TOK, D), BF16),
        in_specs=[pl.BlockSpec(memory_space=pltpu.SMEM)] + [anywhere] * 8,
        out_specs=anywhere,
        scratch_shapes=[pltpu.SemaphoreType.DMA((8,))],
        cost_estimate=pl.CostEstimate(flops=0, bytes_accessed=3 * 10**6, transcendentals=0),
        name="gather_columns",
    )(place, *pieces)


def per_device(h, modulation, wq, wk, wv, mq, mk, mv, gain_q, gain_k):
    xh, z, c, y, xl = (lax.axis_index(a).astype(I32) for a in AXES)
    way = 1 - 2 * c
    blocks = [(s, dx) for dx in range(2) for s in range(4)]
    canonical = jnp.stack([((y - way * s) % Y) * 2 + (xl ^ dx) for s, dx in blocks])
    sources = jnp.stack([((y + way * s) % Y) * 2 + (xl ^ dx) for s, dx in blocks])
    rows = [((z - way * s) % Z) * 2 + c for s in range(4)] + [((z + way * s) % Z) * 2 + 1 - c for s in range(4)]
    place_1 = jnp.concatenate([jnp.stack([xh] + rows), canonical])
    place_2 = jnp.concatenate([jnp.stack([1 - xh] + rows), canonical])
    me = (y * 2 + xl)[None]

    w0 = masked_weights(wq, wk, wv, mq, mk, mv)
    x0 = layer_norm(h, modulation)

    w1 = ring_z(w0)
    p0 = swap_xh(w0)
    x1 = ring_y(x0)
    b0 = swap_xl(x0)
    w2 = ring_z(w1)
    x2 = ring_y(x1)
    w3 = ring_z(w2)
    x3 = ring_y(x2)
    own = [w0, w1, w2, w3]
    own_half = own + [swap_c(w) for w in own]
    p1 = ring_z(p0)
    b1 = ring_y(b0)
    b3 = swap_xl(x3)
    p2 = ring_z(p1)
    b2 = ring_y(b1)
    p3 = ring_z(p2)
    other = [p0, p1, p2, p3]
    other_half = other + [swap_c(w) for w in other]
    xs_a = [x0, x1, x2, x3]
    xs_b = [b0, b1, b2, b3]
    tables = rope_tables(canonical)

    acc_a = project(place_1, xs_a, own_half)
    acc_b = project(place_1, xs_b, own_half)
    product = gram_rows(me, xs_a + xs_b, XH * Z * C * 8 * TOK)
    gram = lax.psum_scatter(product, ("xh", "z", "c"), scatter_dimension=0, tiled=True)
    acc = jnp.concatenate([acc_a, acc_b])
    q, k, v, squares = project(place_2, xs_a + xs_b, other_half, acc, True)
    all_squares = [squares] + [to_owner(squares, s, dx) for s, dx in blocks[1:]]
    outs = attend(canonical, q, k, v, all_squares, gain_q, gain_k, tables)
    pieces = [outs[0]] + [to_owner(o, s, dx) for o, (s, dx) in zip(outs[1:], blocks[1:])]
    return gather_columns(sources, pieces), gram.astype(F32)[None]


def solution(mesh):
    fine = Mesh(mesh.devices.reshape(XH, Z, C, Y, XL), AXES)
    grp, sp = ("xh", "z", "c"), ("y", "xl")
    return jax.shard_map(
        per_device,
        mesh=fine,
        in_specs=(
            P(grp, sp, None),
            P(grp, None, None),
            P(grp, sp),
            P(grp, sp),
            P(grp, sp),
            P(grp, sp),
            P(grp, sp),
            P(grp, sp),
            P(sp),
            P(sp),
        ),
        out_specs=(P(grp, sp, None), P(sp, grp, None)),
        check_vma=False,
    )
```

time: 536 us -> 416 us (0.78); the launches traced: 530 us -> 416 us
  waiting for transfers between devices: 334 us -> 204 us
  Pallas kernels: 0 us -> 126 us
  matrix products: 93.5 us -> 0 us
  blocking collectives: 46.7 us -> 0 us
  starting transfers between devices: 0.2 us -> 39.8 us
    all_gather x4 -> x0, waiting for transfers between devices: 330 us -> none  [the longest x1 195 us: per_device(): gathered = lax.all_gather(normed, 'sp', axis=0, tiled=True)]
    ppermute x0 -> x36, waiting for transfers between devices: none -> 204 us  [permute(): return lax.ppermute(x, AXES, pairs)]
    pallas_call x0 -> x8, Pallas kernels: none -> 126 us  [the longest x3 49.9 us: project(): pl.pallas_call(functools.partial(project_kernel, n_x, first, last), out_s...]
    dot_general x8 -> x0, matrix products: 75.5 us -> none  [the longest x3 38 us: add_rows(): return jnp.dot(gathered, shard_piece, preferred_element_type=jnp.float32)]
    ppermute x0 -> x36, starting transfers between devices: none -> 39.8 us  [permute(): return lax.ppermute(x, AXES, pairs)]
    all_to_all x1 -> x0, blocking collectives: 27.5 us -> none  [per_device(): lax.all_to_all(attended, 'sp', split_axis=0, concat_axis=1, tiled=True)]
    psum x1 -> x0, blocking collectives: 19.1 us -> none  [per_device(): lax.psum((jnp.sum(queries * queries, axis=1), jnp.sum(keys_proj * keys_pr...]
    sub x2 -> x0, matrix products: 18 us -> none  [one_block(): expo_scores = jnp.exp(scores - top_score)]
  transfers between devices with their start and end apart: 5 -> 37, of which waited for: 5 -> 19; matrix products, arithmetic and copies ran while one was open for 23% -> 3% of each run, Pallas kernels for 0% -> 26%
where the time goes in v1:
time: 416 us
  waiting for transfers between devices  204 us (49%)
  Pallas kernels  126 us (30%)
  starting transfers between devices  39.8 us (10%)
  local copies, waits for them, and re-layouts  18.9 us (5%)
  between operations  14.5 us (3%)
  other arithmetic  12.5 us (3%)
    ppermute x36, waiting for transfers between devices, permute(): return lax.ppermute(x, AXES, pairs)  204 us
    pallas_call x3, Pallas kernels, project(): pl.pallas_call(functools.partial(project_kernel, n_x, first, last), out_s...  49.9 us
    pallas_call x1, Pallas kernels, gather_columns(): pl.pallas_call(gather_kernel, out_shape=jax.ShapeDtypeStruct((1, TOK, D),...  41.5 us
    ppermute x36, starting transfers between devices, permute(): return lax.ppermute(x, AXES, pairs)  39.8 us
    unnamed x72, local copies, waits for them, and re-layouts  18 us
    pallas_call x1, Pallas kernels, attend(): pl.pallas_call(attend_kernel, out_shape=(jax.ShapeDtypeStruct((TOK, COLS)...  17.6 us
    pallas_call x1, Pallas kernels, gram_rows(): pl.pallas_call(functools.partial(gram_kernel, tokens), out_shape=jax.Shap...  13.9 us
  transfers between devices with their start and end apart: 37, of which 19 were waited for; matrix products, arithmetic and copies ran while one was open for 3% of the time, Pallas kernels for 26%

profile of v1, /device:TPU:0, one launch (start us, length us, event | category | flops | bytes accessed | tf_op | source)
XLA Modules:
  0.0 415.5 jit_solution(6992995247737787667)
XLA Ops:
  7.2 1.3 copy-done.1
  8.5 0.8 copy-done.15
  9.3 1.7 layer_norm.1.refs_0_
  11.0 1.7 collective-permute-start
  12.8 1.5 collective-permute-start.3
  14.2 15.7 %collective-permute-done.refs_1_ = bf16[128,5120]{1,0:T(8,128)(2,1)S(1)} collective-permute-done((bf16[128,5120]{1,0:T(8,128)(2,1)S(1)}, bf16[128,5120]{1,0:T(8,128)(2,1)S(1)}, u32[]{:S(2)}, u32[]{:S(2)}) %collective-permute-start) | collective-permute-done | bytes 1310752 | tf_op jit(solution)/shard_map/ppermute | solution.py:38
  30.4 1.1 copy-done.2
  31.4 13.0 %collective-permute-done.3.refs_0_.refs_4_ = bf16[128,5120]{1,0:T(8,128)(2,1)S(1)} collective-permute-done((bf16[128,5120]{1,0:T(8,128)(2,1)S(1)}, bf16[128,5120]{1,0:T(8,128)(2,1)S(1)}, u32[]{:S(2)}, u32[]{:S(2)}) %collective-permute-start.3) | collective-permute-done | bytes 1310752 | tf_op jit(solution)/shard_map/ppermute | solution.py:38
  44.4 1.2 copy-done.4
  45.5 3.2 collective-permute-done.1.refs_2_
  48.7 1.1 copy-done.6
  49.8 13.5 %collective-permute-done.4.refs_1_.refs_5_ = bf16[128,5120]{1,0:T(8,128)(2,1)} collective-permute-done((bf16[128,5120]{1,0:T(8,128)(2,1)S(1)}, bf16[128,5120]{1,0:T(8,128)(2,1)}, u32[]{:S(2)}, u32[]{:S(2)}) %collective-permute-start.4) | collective-permute-done | bytes 1310752 | tf_op jit(solution)/shard_map/ppermute | solution.py:38
  63.3 14.0 %collective-permute-done.2.refs_3_ = bf16[128,5120]{1,0:T(8,128)(2,1)} collective-permute-done((bf16[128,5120]{1,0:T(8,128)(2,1)S(1)}, bf16[128,5120]{1,0:T(8,128)(2,1)}, u32[]{:S(2)}, u32[]{:S(2)}) %collective-permute-start.2) | collective-permute-done | bytes 1310752 | tf_op jit(solution)/shard_map/ppermute | solution.py:38
  77.3 1.5 collective-permute-start.6
  78.8 12.6 %collective-permute-done.5.refs_2_.refs_6_ = bf16[128,5120]{1,0:T(8,128)(2,1)} collective-permute-done((bf16[128,5120]{1,0:T(8,128)(2,1)}, bf16[128,5120]{1,0:T(8,128)(2,1)}, u32[]{:S(2)}, u32[]{:S(2)}) %collective-permute-start.5) | collective-permute-done | bytes 1310752 | tf_op jit(solution)/shard_map/ppermute | solution.py:38
  91.4 15.0 %collective-permute-done.6.refs_3_.refs_7_ = bf16[128,5120]{1,0:T(8,128)(2,1)} collective-permute-done((bf16[128,5120]{1,0:T(8,128)(2,1)}, bf16[128,5120]{1,0:T(8,128)(2,1)}, u32[]{:S(2)}, u32[]{:S(2)}) %collective-permute-start.6) | collective-permute-done | bytes 1310752 | tf_op jit(solution)/shard_map/ppermute | solution.py:38
  106.4 1.3 copy-done.3
  107.7 1.3 copy-done.5
  109.1 1.3 copy-done.7
  110.4 13.9 %gram_rows.1 = bf16[640,5120]{1,0:T(8,128)(2,1)} custom-call(s32[1]{0:T(128)} %bitcast.27.place, bf16[128,5120]{1,0:T(8,128)(2,1)S(1)} %layer_norm.1.refs_0_, bf16[128,5120]{1,0:T(8,128)(2,1)S(1)} %copy-done.3, bf16[128,5120]{1,0:T(8,128)(2,1)S(1)} %copy-done.7, bf16[128,5120]{1,0:T(8,128)(2,1)} %collective-permute-done.2.refs_3_, ...), custom_call_target="tpu_custom_call" | custom-call | flops 6710886400 | bytes 17000000 | tf_op jit(solution)/shard_map/gram_rows/pallas_call | solution.py:236
  124.4 0.9 copy-done.8
  125.7 0.9 masked_weights.1.refs_4_
  126.6 3.1 collective-permute-start.7
  129.7 1.9 collective-permute-start.15
  131.7 22.6 %collective-permute-done.7.refs_8_ = bf16[320,1920]{1,0:T(8,128)(2,1)S(1)} collective-permute-done((bf16[320,1920]{1,0:T(8,128)(2,1)S(1)}, bf16[320,1920]{1,0:T(8,128)(2,1)S(1)}, u32[]{:S(2)}, u32[]{:S(2)}) %collective-permute-start.7) | collective-permute-done | bytes 1228832 | tf_op jit(solution)/shard_map/ppermute | solution.py:38
  154.3 1.9 collective-permute-start.8
  156.2 1.9 collective-permute-start.16
  158.1 21.0 %collective-permute-done.8.refs_9_ = bf16[320,1920]{1,0:T(8,128)(2,1)S(1)} collective-permute-done((bf16[320,1920]{1,0:T(8,128)(2,1)S(1)}, bf16[320,1920]{1,0:T(8,128)(2,1)S(1)}, u32[]{:S(2)}, u32[]{:S(2)}) %collective-permute-start.8) | collective-permute-done | bytes 1228832 | tf_op jit(solution)/shard_map/ppermute | solution.py:38
  179.5 19.9 %collective-permute-done.16.refs_6_ = bf16[320,1920]{1,0:T(8,128)(2,1)} collective-permute-done((bf16[320,1920]{1,0:T(8,128)(2,1)S(1)}, bf16[320,1920]{1,0:T(8,128)(2,1)}, u32[]{:S(2)}, u32[]{:S(2)}) %collective-permute-start.16) | collective-permute-done | bytes 1228832 | tf_op jit(solution)/shard_map/ppermute | solution.py:38
  200.1 19.1 %collective-permute-done.9.refs_10_ = bf16[320,1920]{1,0:T(8,128)(2,1)} collective-permute-done((bf16[320,1920]{1,0:T(8,128)(2,1)S(1)}, bf16[320,1920]{1,0:T(8,128)(2,1)}, u32[]{:S(2)}, u32[]{:S(2)}) %collective-permute-start.9) | collective-permute-done | bytes 1228832 | tf_op jit(solution)/shard_map/ppermute | solution.py:38
  219.2 13.2 %collective-permute-done.17.refs_7_ = bf16[320,1920]{1,0:T(8,128)(2,1)} collective-permute-done((bf16[320,1920]{1,0:T(8,128)(2,1)}, bf16[320,1920]{1,0:T(8,128)(2,1)}, u32[]{:S(2)}, u32[]{:S(2)}) %collective-permute-start.17) | collective-permute-done | bytes 1228832 | tf_op jit(solution)/shard_map/ppermute | solution.py:38
  233.9 11.6 %collective-permute-done.10.refs_11_ = bf16[320,1920]{1,0:T(8,128)(2,1)} collective-permute-done((bf16[320,1920]{1,0:T(8,128)(2,1)}, bf16[320,1920]{1,0:T(8,128)(2,1)}, u32[]{:S(2)}, u32[]{:S(2)}) %collective-permute-start.10) | collective-permute-done | bytes 1228832 | tf_op jit(solution)/shard_map/ppermute | solution.py:38
  245.6 13.3 %project_4_1_0.2 = f32[512,1920]{1,0:T(8,128)} custom-call(s32[17]{0:T(128)S(1)} %concatenate.35.place, bf16[128,5120]{1,0:T(8,128)(2,1)} %copy-done, bf16[128,5120]{1,0:T(8,128)(2,1)} %copy-done.2, bf16[128,5120]{1,0:T(8,128)(2,1)} %copy-done.6, bf16[128,5120]{1,0:T(8,128)(2,1)} %collective-permute-done.2.refs_3_, ...), custom_call_target="tpu_custom_call" | custom-call | flops 5033164800 | bytes 15000000 | tf_op jit(solution)/shard_map/project_4_1_0/pallas_call | solution.py:181
  258.9 13.3 %project_4_1_0.3 = f32[512,1920]{1,0:T(8,128)} custom-call(s32[17]{0:T(128)S(1)} %concatenate.35.place, bf16[128,5120]{1,0:T(8,128)(2,1)} %copy-done.4, bf16[128,5120]{1,0:T(8,128)(2,1)} %collective-permute-done.4.refs_1_.refs_5_, bf16[128,5120]{1,0:T(8,128)(2,1)} %collective-permute-done.5.refs_2_.refs_6_, ...), custom_call_target="tpu_custom_call" | custom-call | flops 5033164800 | bytes 15000000 | tf_op jit(solution)/shard_map/project_4_1_0/pallas_call | solution.py:181
  272.2 5.9 %pad_maximum_fusion.refs_16_ = f32[1024,1920]{1,0:T(8,128)} fusion(f32[512,1920]{1,0:T(8,128)} %project_4_1_0.3, f32[512,1920]{1,0:T(8,128)S(1)} %copy-done.23), kind=kLoop, calls=%fused_computation | loop fusion | flops 1966080 | bytes 15728640 | tf_op jit(solution)/shard_map/concatenate | solution.py:414
  278.1 1.0 copy-done.33
  279.5 1.0 copy-done.35
  280.6 23.3 %project_8_0_1.1 = (f32[1024,640]{1,0:T(8,128)}, f32[1024,640]{1,0:T(8,128)}, bf16[1024,640]{1,0:T(8,128)(2,1)}, f32[8,8,128]{2,1,0:T(8,128)S(1)}) custom-call(s32[17]{0:T(128)S(1)} %concatenate.34.place, bf16[128,5120]{1,0:T(8,128)(2,1)} %copy-done, bf16[128,5120]{1,0:T(8,128)(2,1)} %copy-done.2, bf16[128,5120]{1,0:T(8,128)(2,1)} %copy-done.6, ...), custom_call_target="tpu_custom_call" | custom-call | flops 10066329600 | bytes 15000000 | tf_op jit(solution)/shard_map/project_8_0_1/pallas_call | solution.py:181
  303.9 4.4 %collective-permute-start.22 = (f32[8,8,128]{2,1,0:T(8,128)S(1)}, f32[8,8,128]{2,1,0:T(8,128)S(1)}, u32[]{:S(2)}, u32[]{:S(2)}) collective-permute-start(f32[8,8,128]{2,1,0:T(8,128)S(1)} %get-tuple-element.17.refs_0_), channel_id=1, source_target_pairs={{0,6},{1,7},{2,0},{3,1},{4,2},{5,3},{6,4},{7,5},{8,10},{9,11},{10,... | collective-permute-start | bytes 98312 | tf_op jit(solution)/shard_map/ppermute | solution.py:38
  308.3 1.0 collective-permute-start.24
  309.3 1.5 collective-permute-start.25
  310.8 2.3 collective-permute-start.26
  313.1 3.2 collective-permute-start.27
  316.4 4.5 %fusion.2 = (f32[1024,128]{1,0:T(8,128)S(1)}, f32[1024,128]{1,0:T(8,128)S(1)}, f32[1024,128]{1,0:T(8,128)S(1)}) fusion(f32[128]{0:T(128)S(1)} %negate_power_fusion, f32[1024]{0:T(1024)S(1)} %get-tuple-element.31, f32[1024]{0:T(1024)S(1)} %convert_bitcast_fusion, f32[1024]{0:T(1024)S(1)} %get-tuple-element.32, pred[128]{0:T(512)(128)(4,1)S(1)} %get-tuple-element.33, ...), kind=kLoop, calls=%fused_computation.5 | loop fusion | flops 786432 | bytes 1586048 | tf_op jit(solution)/shard_map/jit(_where)/select_n | solution.py:283
  321.0 1.4 collective-permute-done.28.refs_7_
  322.4 1.7 copy-done.20
  324.1 1.7 copy-done.21
  325.9 17.6 %attend.1 = (bf16[128,640]{1,0:T(8,128)(2,1)S(1)}, bf16[128,640]{1,0:T(8,128)(2,1)S(1)}, bf16[128,640]{1,0:T(8,128)(2,1)S(1)}, bf16[128,640]{1,0:T(8,128)(2,1)S(...) custom-call(s32[8]{0:T(128)S(1)} %stack.103.place, ...), custom_call_target="tpu_custom_call" | custom-call | flops 2684354560 | bytes 10000000 | tf_op jit(solution)/shard_map/attend/pallas_call | solution.py:334
  343.5 0.7 copy-done.14
  344.2 1.8 collective-permute-start.29
  346.0 0.9 collective-permute-start.31
  346.8 1.5 collective-permute-start.32
  348.3 2.4 collective-permute-start.33
  350.7 0.6 collective-permute-done.29.refs_1_
  351.3 2.7 collective-permute-start.34
  353.9 1.9 collective-permute-done.30.refs_2_
  355.8 2.2 collective-permute-start.35
  358.0 0.6 stack.96.place
  358.6 0.7 collective-permute-done.33.refs_5_
  359.3 3.0 collective-permute-done.34.refs_6_
  362.3 2.2 collective-permute-done.35.refs_7_
  364.6 0.6 copy-done.30
  365.2 41.5 %gather_columns.1 = bf16[1,128,5120]{2,1,0:T(8,128)(2,1)} custom-call(s32[8]{0:T(128)} %stack.96.place, bf16[128,640]{1,0:T(8,128)(2,1)} %copy-done.14, bf16[128,640]{1,0:T(8,128)(2,1)} %copy-done.24, bf16[128,640]{1,0:T(8,128)(2,1)} %copy-done.25, bf16[128,640]{1,0:T(8,128)(2,1)} %copy-done.26, bf16[128,640]{1,0:T(8,128)(2,1)} %copy-done.27, ...), custom_call_target="tpu_custom_call" | custom-call | bytes 3000000 | tf_op jit(solution)/shard_map/gather_columns/pallas_call | solution.py:363
  406.8 1.9 bitcast_convert_fusion
  (108 shorter events, 4.0 us)
Async XLA Ops:
  7.2 399.6 %reduce-scatter.2.cloned.1.call-start = ((), (), s32[]{:S(2)}) async-start(), calls=%async_computation.1 | async-start | bytes 6963200 | tf_op jit(solution)/shard_map/reduce_scatter | solution.py:413
  7.2 1.3 copy-start.1
  11.0 113.3 %copy-start = (bf16[128,5120]{1,0:T(8,128)(2,1)}, bf16[128,5120]{1,0:T(8,128)(2,1)S(1)}, u32[]{:S(2)}) copy-start(bf16[128,5120]{1,0:T(8,128)(2,1)S(1)} %layer_norm.1.refs_0_) | copy-start | bytes 3932164
  11.0 18.9 %collective-permute-start = (bf16[128,5120]{1,0:T(8,128)(2,1)S(1)}, bf16[128,5120]{1,0:T(8,128)(2,1)S(1)}, u32[]{:S(2)}, u32[]{:S(2)}) collective-permute-start(bf16[128,5120]{1,0:T(8,128)(2,1)S(1)} %layer_norm.1.refs_0_), channel_id=1, source_target_pairs={{0,2},{1,3},{2,4},{3,5},{4,6},{5,7},{6,0},{7,1},{8,14},{9,15},{10,... | collective-permute-start | bytes 3932168 | tf_op jit(solution)/shard_map/ppermute | solution.py:38
  12.8 31.6 %collective-permute-start.3 = (bf16[128,5120]{1,0:T(8,128)(2,1)S(1)}, bf16[128,5120]{1,0:T(8,128)(2,1)S(1)}, u32[]{:S(2)}, u32[]{:S(2)}) collective-permute-start(bf16[128,5120]{1,0:T(8,128)(2,1)S(1)} %layer_norm.1.refs_0_), channel_id=1, source_target_pairs={{0,1},{1,0},{2,3},{3,2},{4,5},{5,4},{6,7},{7,6},{8,9},{9,8},{10,11... | collective-permute-start | bytes 3932168 | tf_op jit(solution)/shard_map/ppermute | solution.py:38
  29.9 18.8 %collective-permute-start.1 = (bf16[128,5120]{1,0:T(8,128)(2,1)S(1)}, bf16[128,5120]{1,0:T(8,128)(2,1)S(1)}, u32[]{:S(2)}, u32[]{:S(2)}) collective-permute-start(bf16[128,5120]{1,0:T(8,128)(2,1)S(1)} %collective-permute-done.refs_1_), channel_id=1, source_target_pairs={{0,2},{1,3},{2,4},{3,5},{4,6},{5,7},{6,0},{7,1},{8,14},{9,15},{10,... | collective-permute-start | bytes 3932168 | tf_op jit(solution)/shard_map/ppermute | solution.py:38
  44.4 18.9 %collective-permute-start.4 = (bf16[128,5120]{1,0:T(8,128)(2,1)S(1)}, bf16[128,5120]{1,0:T(8,128)(2,1)}, u32[]{:S(2)}, u32[]{:S(2)}) collective-permute-start(bf16[128,5120]{1,0:T(8,128)(2,1)S(1)} %collective-permute-done.3.refs_0_.refs_4_), channel_id=1, source_target_pairs={{0,2},{1,3},{2,4},{3,5},{4,6},{5,7},{6,0},{7,1},{8,14},{9,15},{10,... | collective-permute-start | bytes 3932168 | tf_op jit(solution)/shard_map/ppermute | solution.py:38
  44.4 1.2 copy-start.4
  48.7 28.6 %collective-permute-start.2 = (bf16[128,5120]{1,0:T(8,128)(2,1)S(1)}, bf16[128,5120]{1,0:T(8,128)(2,1)}, u32[]{:S(2)}, u32[]{:S(2)}) collective-permute-start(bf16[128,5120]{1,0:T(8,128)(2,1)S(1)} %collective-permute-done.1.refs_2_), channel_id=1, source_target_pairs={{0,2},{1,3},{2,4},{3,5},{4,6},{5,7},{6,0},{7,1},{8,14},{9,15},{10,... | collective-permute-start | bytes 3932168 | tf_op jit(solution)/shard_map/ppermute | solution.py:38
  63.3 28.1 %collective-permute-start.5 = (bf16[128,5120]{1,0:T(8,128)(2,1)}, bf16[128,5120]{1,0:T(8,128)(2,1)}, u32[]{:S(2)}, u32[]{:S(2)}) collective-permute-start(bf16[128,5120]{1,0:T(8,128)(2,1)} %collective-permute-done.4.refs_1_.refs_5_), channel_id=1, source_target_pairs={{0,2},{1,3},{2,4},{3,5},{4,6},{5,7},{6,0},{7,1},{8,14},{9,15},{10,... | collective-permute-start | bytes 3932168 | tf_op jit(solution)/shard_map/ppermute | solution.py:38
  77.3 29.1 %collective-permute-start.6 = (bf16[128,5120]{1,0:T(8,128)(2,1)}, bf16[128,5120]{1,0:T(8,128)(2,1)}, u32[]{:S(2)}, u32[]{:S(2)}) collective-permute-start(bf16[128,5120]{1,0:T(8,128)(2,1)} %collective-permute-done.2.refs_3_), channel_id=1, source_target_pairs={{0,1},{1,0},{2,3},{3,2},{4,5},{5,4},{6,7},{7,6},{8,9},{9,8},{10,11... | collective-permute-start | bytes 3932168 | tf_op jit(solution)/shard_map/ppermute | solution.py:38
  106.4 1.3 copy-start.3
  107.7 1.3 copy-start.5
  109.1 1.3 copy-start.7
  124.3 1.2 copy-start.10
  124.3 1.3 copy-start.11
  124.3 1.3 copy-start.12
  124.4 1.4 copy-start.13
  126.6 27.7 %collective-permute-start.7 = (bf16[320,1920]{1,0:T(8,128)(2,1)S(1)}, bf16[320,1920]{1,0:T(8,128)(2,1)S(1)}, u32[]{:S(2)}, u32[]{:S(2)}) collective-permute-start(bf16[320,1920]{1,0:T(8,128)(2,1)S(1)} %masked_weights.1.refs_4_), channel_id=1, source_target_pairs={{0,64},{1,65},{2,66},{3,67},{4,68},{5,69},{6,70},{7,71},{8,72},{9,... | collective-permute-start | bytes 3686408 | tf_op jit(solution)/shard_map/ppermute | solution.py:38
  129.7 26.5 %collective-permute-start.15 = (bf16[320,1920]{1,0:T(8,128)(2,1)S(1)}, bf16[320,1920]{1,0:T(8,128)(2,1)S(1)}, u32[]{:S(2)}, u32[]{:S(2)}) collective-permute-start(bf16[320,1920]{1,0:T(8,128)(2,1)S(1)} %masked_weights.1.refs_4_), channel_id=1, source_target_pairs={{0,16},{1,17},{2,18},{3,19},{4,20},{5,21},{6,22},{7,23},{8,56},{9,... | collective-permute-start | bytes 3686408 | tf_op jit(solution)/shard_map/ppermute | solution.py:38
  154.3 45.2 %copy-start.16 = (bf16[320,1920]{1,0:T(8,128)(2,1)}, bf16[320,1920]{1,0:T(8,128)(2,1)S(1)}, u32[]{:S(2)}) copy-start(bf16[320,1920]{1,0:T(8,128)(2,1)S(1)} %collective-permute-done.7.refs_8_) | copy-start | bytes 3686404
  154.3 24.9 %collective-permute-start.8 = (bf16[320,1920]{1,0:T(8,128)(2,1)S(1)}, bf16[320,1920]{1,0:T(8,128)(2,1)S(1)}, u32[]{:S(2)}, u32[]{:S(2)}) collective-permute-start(bf16[320,1920]{1,0:T(8,128)(2,1)S(1)} %collective-permute-done.7.refs_8_), channel_id=1, source_target_pairs={{0,16},{1,17},{2,18},{3,19},{4,20},{5,21},{6,22},{7,23},{8,56},{9,... | collective-permute-start | bytes 3686408 | tf_op jit(solution)/shard_map/ppermute | solution.py:38
  156.2 43.3 %collective-permute-start.16 = (bf16[320,1920]{1,0:T(8,128)(2,1)S(1)}, bf16[320,1920]{1,0:T(8,128)(2,1)}, u32[]{:S(2)}, u32[]{:S(2)}) collective-permute-start(bf16[320,1920]{1,0:T(8,128)(2,1)S(1)} %collective-permute-done.15.refs_5_), channel_id=1, source_target_pairs={{0,16},{1,17},{2,18},{3,19},{4,20},{5,21},{6,22},{7,23},{8,56},{9,... | collective-permute-start | bytes 3686408 | tf_op jit(solution)/shard_map/ppermute | solution.py:38
  179.2 20.3 %copy-start.18 = (bf16[320,1920]{1,0:T(8,128)(2,1)}, bf16[320,1920]{1,0:T(8,128)(2,1)S(1)}, u32[]{:S(2)}) copy-start(bf16[320,1920]{1,0:T(8,128)(2,1)S(1)} %collective-permute-done.8.refs_9_) | copy-start | bytes 3686404
  179.2 40.1 %collective-permute-start.9 = (bf16[320,1920]{1,0:T(8,128)(2,1)S(1)}, bf16[320,1920]{1,0:T(8,128)(2,1)}, u32[]{:S(2)}, u32[]{:S(2)}) collective-permute-start(bf16[320,1920]{1,0:T(8,128)(2,1)S(1)} %collective-permute-done.8.refs_9_), channel_id=1, source_target_pairs={{0,16},{1,17},{2,18},{3,19},{4,20},{5,21},{6,22},{7,23},{8,56},{9,... | collective-permute-start | bytes 3686408 | tf_op jit(solution)/shard_map/ppermute | solution.py:38
  199.5 32.9 %collective-permute-start.17 = (bf16[320,1920]{1,0:T(8,128)(2,1)}, bf16[320,1920]{1,0:T(8,128)(2,1)}, u32[]{:S(2)}, u32[]{:S(2)}) collective-permute-start(bf16[320,1920]{1,0:T(8,128)(2,1)} %collective-permute-done.16.refs_6_), channel_id=1, source_target_pairs={{0,16},{1,17},{2,18},{3,19},{4,20},{5,21},{6,22},{7,23},{8,56},{9,... | collective-permute-start | bytes 3686408 | tf_op jit(solution)/shard_map/ppermute | solution.py:38
  199.5 33.4 %collective-permute-start.18 = (bf16[320,1920]{1,0:T(8,128)(2,1)S(1)}, bf16[320,1920]{1,0:T(8,128)(2,1)}, u32[]{:S(2)}, u32[]{:S(2)}) collective-permute-start(bf16[320,1920]{1,0:T(8,128)(2,1)S(1)} %masked_weights.1.refs_4_), channel_id=1, source_target_pairs={{0,8},{1,9},{2,10},{3,11},{4,12},{5,13},{6,14},{7,15},{8,0},{9,1},... | collective-permute-start | bytes 3686408 | tf_op jit(solution)/shard_map/ppermute | solution.py:38
  199.5 33.9 %collective-permute-start.19 = (bf16[320,1920]{1,0:T(8,128)(2,1)S(1)}, bf16[320,1920]{1,0:T(8,128)(2,1)}, u32[]{:S(2)}, u32[]{:S(2)}) collective-permute-start(bf16[320,1920]{1,0:T(8,128)(2,1)S(1)} %collective-permute-done.15.refs_5_), channel_id=1, source_target_pairs={{0,8},{1,9},{2,10},{3,11},{4,12},{5,13},{6,14},{7,15},{8,0},{9,1},... | collective-permute-start | bytes 3686408 | tf_op jit(solution)/shard_map/ppermute | solution.py:38
  200.0 33.5 %collective-permute-start.20 = (bf16[320,1920]{1,0:T(8,128)(2,1)}, bf16[320,1920]{1,0:T(8,128)(2,1)}, u32[]{:S(2)}, u32[]{:S(2)}) collective-permute-start(bf16[320,1920]{1,0:T(8,128)(2,1)} %collective-permute-done.16.refs_6_), channel_id=1, source_target_pairs={{0,8},{1,9},{2,10},{3,11},{4,12},{5,13},{6,14},{7,15},{8,0},{9,1},... | collective-permute-start | bytes 3686408 | tf_op jit(solution)/shard_map/ppermute | solution.py:38
  219.2 26.3 %collective-permute-start.10 = (bf16[320,1920]{1,0:T(8,128)(2,1)}, bf16[320,1920]{1,0:T(8,128)(2,1)}, u32[]{:S(2)}, u32[]{:S(2)}) collective-permute-start(bf16[320,1920]{1,0:T(8,128)(2,1)} %collective-permute-done.9.refs_10_), channel_id=1, source_target_pairs={{0,16},{1,17},{2,18},{3,19},{4,20},{5,21},{6,22},{7,23},{8,56},{9,... | collective-permute-start | bytes 3686408 | tf_op jit(solution)/shard_map/ppermute | solution.py:38
  232.4 13.2 %collective-permute-start.21 = (bf16[320,1920]{1,0:T(8,128)(2,1)}, bf16[320,1920]{1,0:T(8,128)(2,1)}, u32[]{:S(2)}, u32[]{:S(2)}) collective-permute-start(bf16[320,1920]{1,0:T(8,128)(2,1)} %collective-permute-done.17.refs_7_), channel_id=1, source_target_pairs={{0,8},{1,9},{2,10},{3,11},{4,12},{5,13},{6,14},{7,15},{8,0},{9,1},... | collective-permute-start | bytes 3686408 | tf_op jit(solution)/shard_map/ppermute | solution.py:38
  232.9 45.2 %collective-permute-start.11 = (bf16[320,1920]{1,0:T(8,128)(2,1)}, bf16[320,1920]{1,0:T(8,128)(2,1)S(1)}, u32[]{:S(2)}, u32[]{:S(2)}) collective-permute-start(bf16[320,1920]{1,0:T(8,128)(2,1)} %copy-done.16), channel_id=1, source_target_pairs={{0,8},{1,9},{2,10},{3,11},{4,12},{5,13},{6,14},{7,15},{8,0},{9,1},... | collective-permute-start | bytes 3686408 | tf_op jit(solution)/shard_map/ppermute | solution.py:38
  233.4 44.7 %collective-permute-start.12 = (bf16[320,1920]{1,0:T(8,128)(2,1)}, bf16[320,1920]{1,0:T(8,128)(2,1)S(1)}, u32[]{:S(2)}, u32[]{:S(2)}) collective-permute-start(bf16[320,1920]{1,0:T(8,128)(2,1)} %copy-done.18), channel_id=1, source_target_pairs={{0,8},{1,9},{2,10},{3,11},{4,12},{5,13},{6,14},{7,15},{8,0},{9,1},... | collective-permute-start | bytes 3686408 | tf_op jit(solution)/shard_map/ppermute | solution.py:38
  233.5 44.6 %collective-permute-start.13 = (bf16[320,1920]{1,0:T(8,128)(2,1)}, bf16[320,1920]{1,0:T(8,128)(2,1)S(1)}, u32[]{:S(2)}, u32[]{:S(2)}) collective-permute-start(bf16[320,1920]{1,0:T(8,128)(2,1)} %collective-permute-done.9.refs_10_), channel_id=1, source_target_pairs={{0,8},{1,9},{2,10},{3,11},{4,12},{5,13},{6,14},{7,15},{8,0},{9,1},... | collective-permute-start | bytes 3686408 | tf_op jit(solution)/shard_map/ppermute | solution.py:38
  245.6 32.5 %collective-permute-start.14 = (bf16[320,1920]{1,0:T(8,128)(2,1)}, bf16[320,1920]{1,0:T(8,128)(2,1)S(1)}, u32[]{:S(2)}, u32[]{:S(2)}) collective-permute-start(bf16[320,1920]{1,0:T(8,128)(2,1)} %collective-permute-done.10.refs_11_), channel_id=1, source_target_pairs={{0,8},{1,9},{2,10},{3,11},{4,12},{5,13},{6,14},{7,15},{8,0},{9,1},... | collective-permute-start | bytes 3686408 | tf_op jit(solution)/shard_map/ppermute | solution.py:38
  258.8 13.3 %copy-start.23 = (f32[512,1920]{1,0:T(8,128)S(1)}, f32[512,1920]{1,0:T(8,128)}, u32[]{:S(2)}) copy-start(f32[512,1920]{1,0:T(8,128)} %project_4_1_0.2) | copy-start | bytes 11796484
  272.1 8.4 %copy-start.17 = (bf16[320,1920]{1,0:T(8,128)(2,1)S(1)}, bf16[320,1920]{1,0:T(8,128)(2,1)}, u32[]{:S(2)}) copy-start(bf16[320,1920]{1,0:T(8,128)(2,1)} %copy-done.16) | copy-start | bytes 3686404
  272.2 8.4 %copy-start.19 = (bf16[320,1920]{1,0:T(8,128)(2,1)S(1)}, bf16[320,1920]{1,0:T(8,128)(2,1)}, u32[]{:S(2)}) copy-start(bf16[320,1920]{1,0:T(8,128)(2,1)} %copy-done.18) | copy-start | bytes 3686404
  278.1 1.4 copy-start.34
  303.9 17.0 %copy-start.31 = (f32[640]{0:T(1024)S(1)}, f32[640]{0:T(1024)}, u32[]{:S(2)}) copy-start(f32[640]{0:T(1024)} %param.18) | copy-start | bytes 7684
  303.9 17.0 %copy-start.32 = (f32[640]{0:T(1024)S(1)}, f32[640]{0:T(1024)}, u32[]{:S(2)}) copy-start(f32[640]{0:T(1024)} %param.19) | copy-start | bytes 7684
  303.9 18.4 %copy-start.22 = (bf16[1024,640]{1,0:T(8,128)(2,1)S(1)}, bf16[1024,640]{1,0:T(8,128)(2,1)}, u32[]{:S(2)}) copy-start(bf16[1024,640]{1,0:T(8,128)(2,1)} %get-tuple-element.16.v_ref) | copy-start | bytes 3932164
  303.9 9.2 %collective-permute-start.22 = (f32[8,8,128]{2,1,0:T(8,128)S(1)}, f32[8,8,128]{2,1,0:T(8,128)S(1)}, u32[]{:S(2)}, u32[]{:S(2)}) collective-permute-start(f32[8,8,128]{2,1,0:T(8,128)S(1)} %get-tuple-element.17.refs_0_), channel_id=1, source_target_pairs={{0,6},{1,7},{2,0},{3,1},{4,2},{5,3},{6,4},{7,5},{8,10},{9,11},{10,... | collective-permute-start | bytes 98312 | tf_op jit(solution)/shard_map/ppermute | solution.py:38
  308.3 8.0 %collective-permute-start.23 = (f32[8,8,128]{2,1,0:T(8,128)S(1)}, f32[8,8,128]{2,1,0:T(8,128)S(1)}, u32[]{:S(2)}, u32[]{:S(2)}) collective-permute-start(f32[8,8,128]{2,1,0:T(8,128)S(1)} %get-tuple-element.17.refs_0_), channel_id=1, source_target_pairs={{0,4},{1,5},{2,6},{3,7},{4,0},{5,1},{6,2},{7,3},{8,12},{9,13},{10,... | collective-permute-start | bytes 98312 | tf_op jit(solution)/shard_map/ppermute | solution.py:38
  308.3 12.6 %collective-permute-start.24 = (f32[8,8,128]{2,1,0:T(8,128)S(1)}, f32[8,8,128]{2,1,0:T(8,128)S(1)}, u32[]{:S(2)}, u32[]{:S(2)}) collective-permute-start(f32[8,8,128]{2,1,0:T(8,128)S(1)} %get-tuple-element.17.refs_0_), channel_id=1, source_target_pairs={{0,2},{1,3},{2,4},{3,5},{4,6},{5,7},{6,0},{7,1},{8,14},{9,15},{10,... | collective-permute-start | bytes 98312 | tf_op jit(solution)/shard_map/ppermute | solution.py:38
  309.3 11.6 %collective-permute-start.25 = (f32[8,8,128]{2,1,0:T(8,128)S(1)}, f32[8,8,128]{2,1,0:T(8,128)S(1)}, u32[]{:S(2)}, u32[]{:S(2)}) collective-permute-start(f32[8,8,128]{2,1,0:T(8,128)S(1)} %get-tuple-element.17.refs_0_), channel_id=1, source_target_pairs={{0,1},{1,0},{2,3},{3,2},{4,5},{5,4},{6,7},{7,6},{8,9},{9,8},{10,11... | collective-permute-start | bytes 98312 | tf_op jit(solution)/shard_map/ppermute | solution.py:38
  310.8 10.1 %collective-permute-start.26 = (f32[8,8,128]{2,1,0:T(8,128)S(1)}, f32[8,8,128]{2,1,0:T(8,128)S(1)}, u32[]{:S(2)}, u32[]{:S(2)}) collective-permute-start(f32[8,8,128]{2,1,0:T(8,128)S(1)} %get-tuple-element.17.refs_0_), channel_id=1, source_target_pairs={{0,7},{1,6},{2,1},{3,0},{4,3},{5,2},{6,5},{7,4},{8,11},{9,10},{10,... | collective-permute-start | bytes 98312 | tf_op jit(solution)/shard_map/ppermute | solution.py:38
  313.1 7.9 %collective-permute-start.27 = (f32[8,8,128]{2,1,0:T(8,128)S(1)}, f32[8,8,128]{2,1,0:T(8,128)S(1)}, u32[]{:S(2)}, u32[]{:S(2)}) collective-permute-start(f32[8,8,128]{2,1,0:T(8,128)S(1)} %get-tuple-element.17.refs_0_), channel_id=1, source_target_pairs={{0,5},{1,4},{2,7},{3,6},{4,1},{5,0},{6,3},{7,2},{8,13},{9,12},{10,... | collective-permute-start | bytes 98312 | tf_op jit(solution)/shard_map/ppermute | solution.py:38
  316.3 6.0 %collective-permute-start.28 = (f32[8,8,128]{2,1,0:T(8,128)S(1)}, f32[8,8,128]{2,1,0:T(8,128)S(1)}, u32[]{:S(2)}, u32[]{:S(2)}) collective-permute-start(f32[8,8,128]{2,1,0:T(8,128)S(1)} %get-tuple-element.17.refs_0_), channel_id=1, source_target_pairs={{0,3},{1,2},{2,5},{3,4},{4,7},{5,6},{6,1},{7,0},{8,15},{9,14},{10,... | collective-permute-start | bytes 98312 | tf_op jit(solution)/shard_map/ppermute | solution.py:38
  322.4 1.7 copy-start.20
  324.1 1.7 copy-start.21
  344.2 7.1 %collective-permute-start.29 = (bf16[128,640]{1,0:T(8,128)(2,1)S(1)}, bf16[128,640]{1,0:T(8,128)(2,1)S(1)}, u32[]{:S(2)}, u32[]{:S(2)}) collective-permute-start(bf16[128,640]{1,0:T(8,128)(2,1)S(1)} %get-tuple-element.19), channel_id=1, source_target_pairs={{0,6},{1,7},{2,0},{3,1},{4,2},{5,3},{6,4},{7,5},{8,10},{9,11},{10,... | collective-permute-start | bytes 491528 | tf_op jit(solution)/shard_map/ppermute | solution.py:38
  346.0 9.8 %collective-permute-start.30 = (bf16[128,640]{1,0:T(8,128)(2,1)S(1)}, bf16[128,640]{1,0:T(8,128)(2,1)S(1)}, u32[]{:S(2)}, u32[]{:S(2)}) collective-permute-start(bf16[128,640]{1,0:T(8,128)(2,1)S(1)} %get-tuple-element.20), channel_id=1, source_target_pairs={{0,4},{1,5},{2,6},{3,7},{4,0},{5,1},{6,2},{7,3},{8,12},{9,13},{10,... | collective-permute-start | bytes 491528 | tf_op jit(solution)/shard_map/ppermute | solution.py:38
  346.0 12.6 %collective-permute-start.31 = (bf16[128,640]{1,0:T(8,128)(2,1)S(1)}, bf16[128,640]{1,0:T(8,128)(2,1)S(1)}, u32[]{:S(2)}, u32[]{:S(2)}) collective-permute-start(bf16[128,640]{1,0:T(8,128)(2,1)S(1)} %get-tuple-element.21), channel_id=1, source_target_pairs={{0,2},{1,3},{2,4},{3,5},{4,6},{5,7},{6,0},{7,1},{8,14},{9,15},{10,... | collective-permute-start | bytes 491528 | tf_op jit(solution)/shard_map/ppermute | solution.py:38
  346.8 11.8 %collective-permute-start.32 = (bf16[128,640]{1,0:T(8,128)(2,1)S(1)}, bf16[128,640]{1,0:T(8,128)(2,1)S(1)}, u32[]{:S(2)}, u32[]{:S(2)}) collective-permute-start(bf16[128,640]{1,0:T(8,128)(2,1)S(1)} %get-tuple-element.22), channel_id=1, source_target_pairs={{0,1},{1,0},{2,3},{3,2},{4,5},{5,4},{6,7},{7,6},{8,9},{9,8},{10,11... | collective-permute-start | bytes 491528 | tf_op jit(solution)/shard_map/ppermute | solution.py:38
  348.3 11.0 %collective-permute-start.33 = (bf16[128,640]{1,0:T(8,128)(2,1)S(1)}, bf16[128,640]{1,0:T(8,128)(2,1)S(1)}, u32[]{:S(2)}, u32[]{:S(2)}) collective-permute-start(bf16[128,640]{1,0:T(8,128)(2,1)S(1)} %get-tuple-element.23), channel_id=1, source_target_pairs={{0,7},{1,6},{2,1},{3,0},{4,3},{5,2},{6,5},{7,4},{8,11},{9,10},{10,... | collective-permute-start | bytes 491528 | tf_op jit(solution)/shard_map/ppermute | solution.py:38
  351.3 13.3 %copy-start.24 = (bf16[128,640]{1,0:T(8,128)(2,1)}, bf16[128,640]{1,0:T(8,128)(2,1)S(1)}, u32[]{:S(2)}) copy-start(bf16[128,640]{1,0:T(8,128)(2,1)S(1)} %collective-permute-done.29.refs_1_) | copy-start | bytes 491524
  351.3 11.1 %collective-permute-start.34 = (bf16[128,640]{1,0:T(8,128)(2,1)S(1)}, bf16[128,640]{1,0:T(8,128)(2,1)S(1)}, u32[]{:S(2)}, u32[]{:S(2)}) collective-permute-start(bf16[128,640]{1,0:T(8,128)(2,1)S(1)} %get-tuple-element.24), channel_id=1, source_target_pairs={{0,5},{1,4},{2,7},{3,6},{4,1},{5,0},{6,3},{7,2},{8,13},{9,12},{10,... | collective-permute-start | bytes 491528 | tf_op jit(solution)/shard_map/ppermute | solution.py:38
  355.8 8.7 %copy-start.25 = (bf16[128,640]{1,0:T(8,128)(2,1)}, bf16[128,640]{1,0:T(8,128)(2,1)S(1)}, u32[]{:S(2)}) copy-start(bf16[128,640]{1,0:T(8,128)(2,1)S(1)} %collective-permute-done.30.refs_2_) | copy-start | bytes 491524
  355.8 8.7 %collective-permute-start.35 = (bf16[128,640]{1,0:T(8,128)(2,1)S(1)}, bf16[128,640]{1,0:T(8,128)(2,1)S(1)}, u32[]{:S(2)}, u32[]{:S(2)}) collective-permute-start(bf16[128,640]{1,0:T(8,128)(2,1)S(1)} %get-tuple-element.25), channel_id=1, source_target_pairs={{0,3},{1,2},{2,5},{3,4},{4,7},{5,6},{6,1},{7,0},{8,15},{9,14},{10,... | collective-permute-start | bytes 491528 | tf_op jit(solution)/shard_map/ppermute | solution.py:38
  358.6 5.9 %copy-start.26 = (bf16[128,640]{1,0:T(8,128)(2,1)}, bf16[128,640]{1,0:T(8,128)(2,1)S(1)}, u32[]{:S(2)}) copy-start(bf16[128,640]{1,0:T(8,128)(2,1)S(1)} %collective-permute-done.31.refs_3_) | copy-start | bytes 491524
  358.6 5.9 %copy-start.27 = (bf16[128,640]{1,0:T(8,128)(2,1)}, bf16[128,640]{1,0:T(8,128)(2,1)S(1)}, u32[]{:S(2)}) copy-start(bf16[128,640]{1,0:T(8,128)(2,1)S(1)} %collective-permute-done.32.refs_4_) | copy-start | bytes 491524
  359.3 5.2 %copy-start.28 = (bf16[128,640]{1,0:T(8,128)(2,1)}, bf16[128,640]{1,0:T(8,128)(2,1)S(1)}, u32[]{:S(2)}) copy-start(bf16[128,640]{1,0:T(8,128)(2,1)S(1)} %collective-permute-done.33.refs_5_) | copy-start | bytes 491524
  362.3 2.2 copy-start.29
  (9 other events, 8.5 us)
Sparse Core Ops, SparseCore 0:
  124.5 95.5 reduce-scatter.1
